TPU v7x, 256 devices: a whole 4x4x8 slice. The times are simulated.
256 devices in a mesh: seq: 16 (over x, y), dp: 16 (over z, core).
Axes of the slice: x: 4, y: 4, z: 8, core: 2. Of those that a mesh axis runs over, the one named last changes fastest.
Arguments:
- query_rows: bfloat16 [16, 6144, 2048], P('dp', 'seq'), may hold values from -30 to 30
- key_rows: bfloat16 [16, 6144, 2048], P('dp', 'seq'), may hold values from -30 to 30
- value_rows: bfloat16 [16, 6144, 2048], P('dp', 'seq'), may hold values from -6 to 6
- key_tiles: int32 [16, 16, 4], P('dp'), may hold values from 0 to 15, as said below
- tile_counts: int32 [16, 16], P('dp'), may hold values from 2 to 4, as said below
- out_weight: bfloat16 [2048, 3072], P('dp'), may hold values from -0.125 to 0.125
- gate_vector: bfloat16 [16, 3072], P('dp'), may hold values from -4 to 4
Outputs:
- gated_out: bfloat16 [16, 6144, 3072], P('dp', 'seq')
Inputs may be any that keep to these rules, and one draw needn't show every extreme that they name: `key_tiles`: in each row of a video the 4 entries are distinct tiles of that video; only the first tile_counts entries are used. `tile_counts`: each video has some query tile that uses all 4 slots.
All inputs are finite; a program needn't handle non-finite values.
Results may differ from a plain program's by a relative error of at most 0.007.
Values may be sent and summed in bfloat16 or wider, within the bound.
A program may use at most 128 MiB of HBM per device.

v0:
```python
import math
import jax
import jax.numpy as jnp
from jax import lax
from jax.sharding import PartitionSpec as P

HD = 128
TILE = 384
MAXK = 4


def attend_local(query_heads, key_heads, value_heads, tile_list, tile_count):
    tile_total = query_heads.shape[0] // TILE
    heads_here = query_heads.shape[1] // HD
    query_tiles = query_heads.reshape(tile_total, TILE, heads_here, HD)
    key_blocks = key_heads.reshape(tile_total, TILE, heads_here, HD)
    value_blocks = value_heads.reshape(tile_total, TILE, heads_here, HD)
    score_scale = 1.0 / math.sqrt(HD)
    running_max = jnp.full((tile_total, heads_here, TILE, 1), -jnp.inf, jnp.float32)
    running_sum = jnp.zeros((tile_total, heads_here, TILE, 1), jnp.float32)
    accumulated = jnp.zeros((tile_total, TILE, heads_here, HD), jnp.float32)
    for key_slot in range(MAXK):
        chosen = tile_list[:, key_slot]
        key_chosen = jnp.take(key_blocks, chosen, axis=0)
        value_chosen = jnp.take(value_blocks, chosen, axis=0)
        scores = (
            jnp.einsum(
                "athd,ashd->ahts", query_tiles, key_chosen, preferred_element_type=jnp.float32
            )
            * score_scale
        )
        is_live = (key_slot < tile_count)[:, None, None, None]
        scores = jnp.where(is_live, scores, -jnp.inf)
        new_max = jnp.maximum(running_max, jnp.max(scores, axis=-1, keepdims=True))
        factor = jnp.exp(running_max - new_max)
        weights = jnp.exp(scores - new_max)
        running_sum = running_sum * factor + jnp.sum(weights, axis=-1, keepdims=True)
        added = jnp.einsum(
            "ahts,ashd->athd",
            weights.astype(jnp.bfloat16),
            value_chosen,
            preferred_element_type=jnp.float32,
        )
        accumulated = accumulated * jnp.transpose(factor, (0, 2, 1, 3)) + added
        running_max = new_max
    result = accumulated / jnp.transpose(running_sum, (0, 2, 1, 3))
    return result.reshape(tile_total * TILE, heads_here * HD).astype(jnp.bfloat16)


def shards(query_rows, key_rows, value_rows, key_tiles, tile_counts, out_weight, gate_vector):
    query_heads, key_heads, value_heads = (
        lax.all_to_all(query_rows[0], "seq", split_axis=1, concat_axis=0, tiled=True),
        lax.all_to_all(key_rows[0], "seq", split_axis=1, concat_axis=0, tiled=True),
        lax.all_to_all(value_rows[0], "seq", split_axis=1, concat_axis=0, tiled=True),
    )
    head_result = attend_local(query_heads, key_heads, value_heads, key_tiles[0], tile_counts[0])
    attended = lax.all_to_all(head_result, "seq", split_axis=0, concat_axis=1, tiled=True)
    projected = jnp.dot(
        attended,
        lax.all_gather(out_weight, "dp", axis=0, tiled=True),
        preferred_element_type=jnp.float32,
    )
    gated = gate_vector[0].astype(jnp.float32)[None, :] * projected
    return gated.astype(jnp.bfloat16)[None]


def solution(mesh):
    in_specs = (
        P("dp", "seq", None),
        P("dp", "seq", None),
        P("dp", "seq", None),
        P("dp", None, None),
        P("dp", None),
        P("dp", None),
        P("dp", None),
    )
    out_specs = P("dp", "seq", None)
    return jax.shard_map(shards, mesh=mesh, in_specs=in_specs, out_specs=out_specs, check_vma=False)
```

profile of v0, /device:TPU:96, one launch (start us, length us, event | category | flops | bytes accessed | tf_op | source)
XLA Modules:
  0.0 184.4 jit_solution(7563084368427351228)
XLA Ops:
  10.8 7.0 %all-to-all-start = ((bf16[384,16,128]{2,0,1:T(8,128)(2,1)}), bf16[384,16,128]{2,0,1:T(8,128)(2,1)S(1)}, u32[]{:S(2)}, u32[]{:S(2)}) async-start(bf16[384,16,128]{2,0,1:T(8,128)(2,1)} %copy.23), calls=%async_computation | async-start | bytes 3145728 | tf_op jit(solution)/shard_map/all_to_all | solution.py:53
  21.3 20.2 %all-to-all-done = bf16[384,16,128]{2,0,1:T(8,128)(2,1)S(1)} async-done(((bf16[384,16,128]{2,0,1:T(8,128)(2,1)}), bf16[384,16,128]{2,0,1:T(8,128)(2,1)S(1)}, u32[]{:S(2)}, u32[]{:S(2)}) %all-to-all-start) | async-done | bytes 1572896 | tf_op jit(solution)/shard_map/all_to_all | solution.py:53
  41.6 3.9 %all-to-all-start.2 = ((bf16[384,16,128]{2,0,1:T(8,128)(2,1)}), bf16[384,16,128]{2,0,1:T(8,128)(2,1)S(1)}, u32[]{:S(2)}, u32[]{:S(2)}) async-start(bf16[384,16,128]{2,0,1:T(8,128)(2,1)} %copy.27), calls=%async_computation.2 | async-start | bytes 3145728 | tf_op jit(solution)/shard_map/all_to_all | solution.py:54
  45.5 2.6 %copy.24 = bf16[1,384,2048]{1,2,0:T(8,128)(2,1)} copy(bf16[1,384,2048]{2,1,0:T(8,128)(2,1)} %param.9) | data formatting | bytes 3145728 | tf_op args[0]
  48.1 2.6 %copy.25 = bf16[384,16,128]{2,0,1:T(8,128)(2,1)} copy(bf16[384,16,128]{0,2,1:T(8,128)(2,1)} %bitcast.239) | data formatting | bytes 3145728 | tf_op jit(solution)/shard_map/all_to_all | solution.py:52
  50.7 16.4 %all-to-all-done.2 = bf16[384,16,128]{2,0,1:T(8,128)(2,1)S(1)} async-done(((bf16[384,16,128]{2,0,1:T(8,128)(2,1)}), bf16[384,16,128]{2,0,1:T(8,128)(2,1)S(1)}, u32[]{:S(2)}, u32[]{:S(2)}) %all-to-all-start.2) | async-done | bytes 1572896 | tf_op jit(solution)/shard_map/all_to_all | solution.py:54
  67.1 4.6 %all-to-all-start.1 = ((bf16[384,16,128]{2,0,1:T(8,128)(2,1)}), bf16[384,16,128]{2,0,1:T(8,128)(2,1)}, u32[]{:S(2)}, u32[]{:S(2)}) async-start(bf16[384,16,128]{2,0,1:T(8,128)(2,1)} %copy.25), calls=%async_computation.1 | async-start | bytes 3145728 | tf_op jit(solution)/shard_map/all_to_all | solution.py:52
  77.6 2.0 %gather_fusion.5 = bf16[16,384,128]{2,1,0:T(8,128)(2,1)} fusion(bf16[16,384,128]{2,1,0:T(8,128)(2,1)S(1)} %bitcast.234, s32[1024]{0:T(1024)S(1)} %pad_clamp_fusion.1), kind=kCustom, calls=%fused_computation.5.clone | custom fusion | bytes 3145792 | tf_op jit(solution)/shard_map/jit(_take)/gather | solution.py:25
  83.3 1.9 %gather_fusion = bf16[16,384,128]{2,1,0:T(8,128)(2,1)} fusion(bf16[16,384,128]{2,1,0:T(8,128)(2,1)S(1)} %bitcast.232, s32[1024]{0:T(1024)S(1)} %pad_clamp_fusion.3), kind=kCustom, calls=%fused_computation.clone | custom fusion | bytes 3145792 | tf_op jit(solution)/shard_map/jit(_take)/gather | solution.py:24
  85.2 2.0 %gather_fusion.1 = bf16[16,384,128]{2,1,0:T(8,128)(2,1)} fusion(bf16[16,384,128]{2,1,0:T(8,128)(2,1)S(1)} %bitcast.236, s32[1024]{0:T(1024)S(1)} %pad_clamp_fusion.3), kind=kCustom, calls=%fused_computation.1.clone | custom fusion | bytes 3145792 | tf_op jit(solution)/shard_map/jit(_take)/gather | solution.py:25
  87.2 4.9 %all-to-all-done.1 = bf16[384,16,128]{2,0,1:T(8,128)(2,1)} async-done(((bf16[384,16,128]{2,0,1:T(8,128)(2,1)}), bf16[384,16,128]{2,0,1:T(8,128)(2,1)}, u32[]{:S(2)}, u32[]{:S(2)}) %all-to-all-start.1) | async-done | bytes 1572896 | tf_op jit(solution)/shard_map/all_to_all | solution.py:52
  92.1 3.0 %bitcast_reduce_fusion.1 = (f32[16,384]{1,0:T(8,128)S(1)}, f32[16,384,384]{2,1,0:T(8,128)S(1)}) fusion(pred[16]{0:T(512)(128)(4,1)S(1)} %get-tuple-element.31, bf16[384,16,128]{2,0,1:T(8,128)(2,1)} %all-to-all-done.1, bf16[16,384,128]{2,1,0:T(8,128)(2,1)S(1)} %copy-done.6, pred[16]{0:T(512)(128)(4,1)S(1)} %get-tuple-element.24), kind=kOutput, calls=%fused_computation.12 | convolution fusion | flops 611837952 | bytes 12607520 | tf_op jit(solution)/shard_map/athd,ashd->ahts/dot_general | solution.py:27
  95.1 6.5 %bitcast_reduce_fusion = (f32[16,384]{1,0:T(8,128)S(1)}, f32[16,384,384]{2,1,0:T(8,128)}) fusion(pred[16]{0:T(512)(128)(4,1)S(1)} %get-tuple-element.30, bf16[384,16,128]{2,0,1:T(8,128)(2,1)} %all-to-all-done.1, bf16[16,384,128]{2,1,0:T(8,128)(2,1)S(1)} %copy-done.5, pred[16]{0:T(512)(128)(4,1)S(1)} %get-tuple-element.22), kind=kOutput, calls=%fused_computation.9 | convolution fusion | flops 611837952 | bytes 12607520 | tf_op jit(solution)/shard_map/athd,ashd->ahts/dot_general | solution.py:27
  101.6 3.0 %bitcast_reduce_fusion.3 = (f32[16,384]{1,0:T(8,128)S(1)}, f32[16,384,384]{2,1,0:T(8,128)S(1)}) fusion(pred[16]{0:T(512)(128)(4,1)S(1)} %get-tuple-element.29, bf16[384,16,128]{2,0,1:T(8,128)(2,1)} %all-to-all-done.1, bf16[16,384,128]{2,1,0:T(8,128)(2,1)S(1)} %copy-done.7, pred[16]{0:T(512)(128)(4,1)S(1)} %get-tuple-element.26), kind=kOutput, calls=%fused_computation.18 | convolution fusion | flops 611837952 | bytes 12607520 | tf_op jit(solution)/shard_map/athd,ashd->ahts/dot_general | solution.py:27
  104.6 2.9 %bitcast_reduce_fusion.2 = (f32[16,384]{1,0:T(8,128)S(1)}, f32[16,384,384]{2,1,0:T(8,128)S(1)}) fusion(pred[16]{0:T(512)(128)(4,1)S(1)} %get-tuple-element.28, bf16[384,16,128]{2,0,1:T(8,128)(2,1)} %all-to-all-done.1, bf16[16,384,128]{2,1,0:T(8,128)(2,1)S(1)} %copy-done.4, pred[16]{0:T(512)(128)(4,1)S(1)} %get-tuple-element.15), kind=kOutput, calls=%fused_computation.15 | convolution fusion | flops 611837952 | bytes 12607520 | tf_op jit(solution)/shard_map/athd,ashd->ahts/dot_general | solution.py:27
  107.5 4.0 %fusion.4 = (f32[16,384]{1,0:T(8,128)S(1)}, f32[16,384]{1,0:T(8,128)S(1)}) fusion(f32[16,384,384]{2,1,0:T(8,128)S(1)} %get-tuple-element.37, f32[16,384]{1,0:T(8,128)S(1)} %get-tuple-element.36, pred[16]{0:T(512)(128)(4,1)S(1)} %get-tuple-element.29, f32[16,384]{1,0:T(8,128)S(1)} %get-tuple-element.12, f32[16,384,384]{2,1,0:T(8,128)S(1)} %get-tuple-element.39, ...), kind=kLoop, calls=%fused_computation.24 | loop fusion | flops 18862080 | bytes 18972704 | tf_op jit(solution)/shard_map/reduce_sum | solution.py:37
  111.5 6.7 %fusion.8 = (f32[16,384]{1,0:T(8,128)S(1)}, f32[16,384]{1,0:T(8,128)S(1)}) fusion(f32[16,384,384]{2,1,0:T(8,128)S(1)} %get-tuple-element.35, f32[16,384]{1,0:T(8,128)S(1)} %get-tuple-element.11, pred[16]{0:T(512)(128)(4,1)S(1)} %get-tuple-element.31, f32[16,384]{1,0:T(8,128)S(1)} %get-tuple-element.10, f32[16,384,384]{2,1,0:T(8,128)} %get-tuple-element.33, ...), kind=kLoop, calls=%fused_computation.28 | loop fusion | flops 18862080 | bytes 18972704 | tf_op jit(solution)/shard_map/reduce_sum | solution.py:37
  118.2 7.9 %fusion.12 = f32[16,128,384]{2,1,0:T(8,128)} fusion(f32[16,384,384]{2,1,0:T(8,128)} %get-tuple-element.33, f32[16,384]{1,0:T(8,128)S(1)} %get-tuple-element.10, pred[16]{0:T(512)(128)(4,1)S(1)} %get-tuple-element.30, bf16[16,384,128]{2,1,0:T(8,128)(2,1)S(1)} %copy-done.3, pred[16]{0:T(512)(128)(4,1)S(1)} %get-tuple-element.22), kind=kOutput, calls=%fused_computation.32 | convolution fusion | flops 614203392 | bytes 14180384 | tf_op jit(solution)/shard_map/ahts,ashd->athd/dot_general | solution.py:38
  126.2 3.9 %fusion.14 = f32[16,128,384]{2,1,0:T(8,128)} fusion(f32[16,384,384]{2,1,0:T(8,128)S(1)} %get-tuple-element.35, f32[16,384]{1,0:T(8,128)S(1)} %get-tuple-element.11, pred[16]{0:T(512)(128)(4,1)S(1)} %get-tuple-element.31, bf16[16,384,128]{2,1,0:T(8,128)(2,1)S(1)} %copy-done.2, pred[16]{0:T(512)(128)(4,1)S(1)} %get-tuple-element.24), kind=kOutput, calls=%fused_computation.33 | convolution fusion | flops 614203392 | bytes 14180384 | tf_op jit(solution)/shard_map/ahts,ashd->athd/dot_general | solution.py:38
  130.0 3.9 %fusion.16 = f32[16,128,384]{2,1,0:T(8,128)} fusion(f32[16,384,384]{2,1,0:T(8,128)S(1)} %get-tuple-element.39, f32[16,384]{1,0:T(8,128)S(1)} %get-tuple-element.12, pred[16]{0:T(512)(128)(4,1)S(1)} %get-tuple-element.28, bf16[16,384,128]{2,1,0:T(8,128)(2,1)S(1)} %copy-done.1, pred[16]{0:T(512)(128)(4,1)S(1)} %get-tuple-element.15), kind=kOutput, calls=%fused_computation.34 | convolution fusion | flops 614203392 | bytes 14180384 | tf_op jit(solution)/shard_map/ahts,ashd->athd/dot_general | solution.py:38
  133.9 6.6 %fusion.68 = bf16[16,384,128]{1,2,0:T(8,128)(2,1)} fusion(f32[16,384]{1,0:T(8,128)S(1)} %get-tuple-element.6, f32[16,128,384]{2,1,0:T(8,128)} %fusion.12, f32[16,384]{1,0:T(8,128)S(1)} %get-tuple-element.9, f32[16,128,384]{2,1,0:T(8,128)} %fusion.14, f32[16,384]{1,0:T(8,128)S(1)} %get-tuple-element.8, f32[16,128,384]{2,1,0:T(8,128)} %fusion.16, ...), kind=kOutput, calls=%fused_computation.95 | convolution fusion | flops 621281280 | bytes 22167584 | tf_op jit(solution)/shard_map/ahts,ashd->athd/dot_general | solution.py:38
  140.6 3.8 %all-to-all-start.3 = ((bf16[16,384,128]{1,2,0:T(8,128)(2,1)}), bf16[16,384,128]{1,2,0:T(8,128)(2,1)S(1)}, u32[]{:S(2)}, u32[]{:S(2)}) async-start(bf16[16,384,128]{1,2,0:T(8,128)(2,1)} %fusion.68), calls=%async_computation.3 | async-start | bytes 3145728 | tf_op jit(solution)/shard_map/all_to_all | solution.py:57
  144.5 22.0 %all-to-all-done.3 = bf16[16,384,128]{1,2,0:T(8,128)(2,1)S(1)} async-done(((bf16[16,384,128]{1,2,0:T(8,128)(2,1)}), bf16[16,384,128]{1,2,0:T(8,128)(2,1)S(1)}, u32[]{:S(2)}, u32[]{:S(2)}) %all-to-all-start.3) | async-done | bytes 1572896 | tf_op jit(solution)/shard_map/all_to_all | solution.py:57
  166.5 11.0 %fusion.36 = bf16[1,384,3072]{2,1,0:T(8,128)(2,1)} fusion(bf16[384,2048]{0,1:T(8,128)(2,1)S(1)} %bitcast.240, bf16[2048,3072]{1,0:T(8,128)(2,1)} %all-gather.2.cloned.1.call-done, f32[3072]{0:T(1024)S(1)} %bitcast.241), kind=kOutput, calls=%fused_computation.53 | convolution fusion | flops 4834197504 | bytes 16527360 | tf_op jit(solution)/shard_map/dot_general | solution.py:58
  (43 shorter events, 17.4 us)
Async XLA Ops:
  6.5 160.0 %all-gather.2.cloned.1.call-start = ((), (), s32[]{:S(2)}) async-start(), calls=%async_computation.4 | async-start | bytes 13369344 | tf_op jit(solution)/shard_map/all_gather | solution.py:60
  10.8 30.8 %all-to-all-start = ((bf16[384,16,128]{2,0,1:T(8,128)(2,1)}), bf16[384,16,128]{2,0,1:T(8,128)(2,1)S(1)}, u32[]{:S(2)}, u32[]{:S(2)}) async-start(bf16[384,16,128]{2,0,1:T(8,128)(2,1)} %copy.23), calls=%async_computation | async-start | bytes 3145728 | tf_op jit(solution)/shard_map/all_to_all | solution.py:53
  41.6 25.6 %all-to-all-start.2 = ((bf16[384,16,128]{2,0,1:T(8,128)(2,1)}), bf16[384,16,128]{2,0,1:T(8,128)(2,1)S(1)}, u32[]{:S(2)}, u32[]{:S(2)}) async-start(bf16[384,16,128]{2,0,1:T(8,128)(2,1)} %copy.27), calls=%async_computation.2 | async-start | bytes 3145728 | tf_op jit(solution)/shard_map/all_to_all | solution.py:54
  48.1 23.7 %copy-start.9 = (s32[1,16,4]{1,2,0:T(4,128)S(1)}, s32[1,16,4]{1,2,0:T(4,128)}, u32[]{:S(2)}) copy-start(s32[1,16,4]{1,2,0:T(4,128)} %param.12) | copy-start | bytes 772
  48.1 23.8 %copy-start.10 = (s32[1,16]{1,0:T(1,128)S(1)}, s32[1,16]{1,0:T(1,128)}, u32[]{:S(2)}) copy-start(s32[1,16]{1,0:T(1,128)} %param.13) | copy-start | bytes 196
  67.1 25.0 %all-to-all-start.1 = ((bf16[384,16,128]{2,0,1:T(8,128)(2,1)}), bf16[384,16,128]{2,0,1:T(8,128)(2,1)}, u32[]{:S(2)}, u32[]{:S(2)}) async-start(bf16[384,16,128]{2,0,1:T(8,128)(2,1)} %copy.25), calls=%async_computation.1 | async-start | bytes 3145728 | tf_op jit(solution)/shard_map/all_to_all | solution.py:52
  85.2 6.9 %copy-start.6 = (bf16[16,384,128]{2,1,0:T(8,128)(2,1)S(1)}, bf16[16,384,128]{2,1,0:T(8,128)(2,1)}, u32[]{:S(2)}) copy-start(bf16[16,384,128]{2,1,0:T(8,128)(2,1)} %gather_fusion.4) | copy-start | bytes 4718596
  92.1 3.0 %copy-start.5 = (bf16[16,384,128]{2,1,0:T(8,128)(2,1)S(1)}, bf16[16,384,128]{2,1,0:T(8,128)(2,1)}, u32[]{:S(2)}) copy-start(bf16[16,384,128]{2,1,0:T(8,128)(2,1)} %gather_fusion.6) | copy-start | bytes 4718596
  95.1 6.5 %copy-start.7 = (bf16[16,384,128]{2,1,0:T(8,128)(2,1)S(1)}, bf16[16,384,128]{2,1,0:T(8,128)(2,1)}, u32[]{:S(2)}) copy-start(bf16[16,384,128]{2,1,0:T(8,128)(2,1)} %gather_fusion) | copy-start | bytes 4718596
  101.6 3.0 %copy-start.4 = (bf16[16,384,128]{2,1,0:T(8,128)(2,1)S(1)}, bf16[16,384,128]{2,1,0:T(8,128)(2,1)}, u32[]{:S(2)}) copy-start(bf16[16,384,128]{2,1,0:T(8,128)(2,1)} %gather_fusion.2) | copy-start | bytes 4718596
  111.5 6.7 %copy-start.3 = (bf16[16,384,128]{2,1,0:T(8,128)(2,1)S(1)}, bf16[16,384,128]{2,1,0:T(8,128)(2,1)}, u32[]{:S(2)}) copy-start(bf16[16,384,128]{2,1,0:T(8,128)(2,1)} %gather_fusion.7) | copy-start | bytes 4718596
  118.2 8.0 %copy-start.2 = (bf16[16,384,128]{2,1,0:T(8,128)(2,1)S(1)}, bf16[16,384,128]{2,1,0:T(8,128)(2,1)}, u32[]{:S(2)}) copy-start(bf16[16,384,128]{2,1,0:T(8,128)(2,1)} %gather_fusion.5) | copy-start | bytes 4718596
  126.2 3.9 %copy-start.1 = (bf16[16,384,128]{2,1,0:T(8,128)(2,1)S(1)}, bf16[16,384,128]{2,1,0:T(8,128)(2,1)}, u32[]{:S(2)}) copy-start(bf16[16,384,128]{2,1,0:T(8,128)(2,1)} %gather_fusion.3) | copy-start | bytes 4718596
  130.0 3.9 %copy-start = (bf16[16,384,128]{2,1,0:T(8,128)(2,1)S(1)}, bf16[16,384,128]{2,1,0:T(8,128)(2,1)}, u32[]{:S(2)}) copy-start(bf16[16,384,128]{2,1,0:T(8,128)(2,1)} %gather_fusion.1) | copy-start | bytes 4718596
  140.6 3.9 %copy-start.8 = (bf16[1,3072]{1,0:T(2,128)(2,1)S(1)}, bf16[1,3072]{1,0:T(2,128)(2,1)}, u32[]{:S(2)}) copy-start(bf16[1,3072]{1,0:T(2,128)(2,1)} %param.15) | copy-start | bytes 18436
  140.6 25.9 %all-to-all-start.3 = ((bf16[16,384,128]{1,2,0:T(8,128)(2,1)}), bf16[16,384,128]{1,2,0:T(8,128)(2,1)S(1)}, u32[]{:S(2)}, u32[]{:S(2)}) async-start(bf16[16,384,128]{1,2,0:T(8,128)(2,1)} %fusion.68), calls=%async_computation.3 | async-start | bytes 3145728 | tf_op jit(solution)/shard_map/all_to_all | solution.py:57
Sparse Core Ops, SparseCore 0:
  9.2 76.8 all-gather.1
where the time goes:
time: 185 us; the launch traced here: 184 us
  waiting for transfers between devices  64.4 us (35%)
  matrix products  48.7 us (26%)
  local copies, waits for them, and re-layouts  27.6 us (15%)
  starting transfers between devices  19.4 us (10%)
  between operations  13.6 us (7%)
  other arithmetic  10.8 us (6%)
    dot_general x4, matrix products, attend_local(): jnp.einsum('ahts,ashd->athd', weights.astype(jnp.bfloat16), value_chosen,...  22.4 us
    all_to_all x1, waiting for transfers between devices, shards(): lax.all_to_all(head_result, 'seq', split_axis=0, concat_axis=1, tiled=True)  22 us
    all_to_all x1, waiting for transfers between devices, shards(): lax.all_to_all(key_rows[0], 'seq', split_axis=1, concat_axis=0, tiled=True)  20.2 us
    all_to_all x1, waiting for transfers between devices, shards(): lax.all_to_all(value_rows[0], 'seq', split_axis=1, concat_axis=0, tiled=T...  16.4 us
    dot_general x4, matrix products, attend_local(): jnp.einsum('athd,ashd->ahts', query_tiles, key_chosen, preferred_element_...  15.3 us
    dot_general x1, matrix products, shards(): jnp.dot(attended, lax.all_gather(out_weight, 'dp', axis=0, tiled=True), p...  11 us
    reduce_sum x2, other arithmetic, attend_local(): jnp.sum(weights, axis=-1, keepdims=True)  10.7 us
    gather x4, local copies, waits for them, and re-layouts, attend_local(): value_chosen = jnp.take(value_blocks, chosen, axis=0)  7.72 us
  transfers between devices with their start and end apart: 5, of which 4 were waited for; matrix products, arithmetic and copies ran while one was open for 41% of the time, Pallas kernels for 0%

commit v1 on v0

--- a/solution.py
+++ b/solution.py
@@ -50,7 +50,12 @@
 def shards(query_rows, key_rows, value_rows, key_tiles, tile_counts, out_weight, gate_vector):
     query_heads, key_heads, value_heads = (
         lax.all_to_all(query_rows[0], "seq", split_axis=1, concat_axis=0, tiled=True),
-        lax.all_to_all(key_rows[0], "seq", split_axis=1, concat_axis=0, tiled=True),
+        jnp.concatenate(
+            lax.all_to_all(
+                jnp.stack(jnp.split(key_rows[0], lax.axis_size("seq"), axis=1)), "seq", 0, 0
+            ),
+            axis=0,
+        ),
         lax.all_to_all(value_rows[0], "seq", split_axis=1, concat_axis=0, tiled=True),
     )
     head_result = attend_local(query_heads, key_heads, value_heads, key_tiles[0], tile_counts[0])

time: 185 us -> 196 us (1.059)
  local copies, waits for them, and re-layouts: 27.6 us -> 37.2 us
    unnamed x25 -> x37, local copies, waits for them, and re-layouts: 6.39 us -> 18 us
  transfers between devices with their start and end apart: 5 -> 5, of which waited for: 4 -> 4; matrix products, arithmetic and copies ran while one was open for 41% -> 44% of each run, Pallas kernels for 0% -> 0%
where the time goes in v1:
time: 196 us; the launch traced here: 195 us
  waiting for transfers between devices  65.5 us (33%)
  matrix products  49 us (25%)
  local copies, waits for them, and re-layouts  37.2 us (19%)
  starting transfers between devices  19.3 us (10%)
  between operations  13.6 us (7%)
  other arithmetic  10.8 us (6%)
    dot_general x4, matrix products, attend_local(): jnp.einsum('ahts,ashd->athd', weights.astype(jnp.bfloat16), value_chosen,...  22.4 us
    all_to_all x1, waiting for transfers between devices, shards(): lax.all_to_all(head_result, 'seq', split_axis=0, concat_axis=1, tiled=True)  22.1 us
    all_to_all x1, waiting for transfers between devices, shards(): lax.all_to_all(jnp.stack(jnp.split(key_rows[0], lax.axis_size('seq'), axi...  20.2 us
    unnamed x37, local copies, waits for them, and re-layouts  18 us
    all_to_all x1, waiting for transfers between devices, shards(): lax.all_to_all(value_rows[0], 'seq', split_axis=1, concat_axis=0, tiled=T...  16.5 us
    dot_general x4, matrix products, attend_local(): jnp.einsum('athd,ashd->ahts', query_tiles, key_chosen, preferred_element_...  15.7 us
    dot_general x1, matrix products, shards(): jnp.dot(attended, lax.all_gather(out_weight, 'dp', axis=0, tiled=True), p...  11 us
    reduce_sum x2, other arithmetic, attend_local(): jnp.sum(weights, axis=-1, keepdims=True)  10.7 us
  transfers between devices with their start and end apart: 5, of which 4 were waited for; matrix products, arithmetic and copies ran while one was open for 44% of the time, Pallas kernels for 0%

profile of v1, /device:TPU:96, one launch (start us, length us, event | category | flops | bytes accessed | tf_op | source)
XLA Modules:
  0.0 195.4 jit_solution(4127742209985140750)
XLA Ops:
  21.4 7.0 %all-to-all-start = ((bf16[16,384,128]{2,1,0:T(8,128)(2,1)}), bf16[16,384,128]{2,1,0:T(8,128)(2,1)S(1)}, u32[]{:S(2)}, u32[]{:S(2)}) async-start(bf16[16,384,128]{2,1,0:T(8,128)(2,1)} %fusion.81), calls=%async_computation | async-start | bytes 3145728 | tf_op jit(solution)/shard_map/all_to_all | solution.py:54
  32.0 20.2 %all-to-all-done = bf16[16,384,128]{2,1,0:T(8,128)(2,1)S(1)} async-done(((bf16[16,384,128]{2,1,0:T(8,128)(2,1)}), bf16[16,384,128]{2,1,0:T(8,128)(2,1)S(1)}, u32[]{:S(2)}, u32[]{:S(2)}) %all-to-all-start) | async-done | bytes 1572896 | tf_op jit(solution)/shard_map/all_to_all | solution.py:54
  52.2 3.9 %all-to-all-start.2 = ((bf16[384,16,128]{2,0,1:T(8,128)(2,1)}), bf16[384,16,128]{2,0,1:T(8,128)(2,1)S(1)}, u32[]{:S(2)}, u32[]{:S(2)}) async-start(bf16[384,16,128]{2,0,1:T(8,128)(2,1)} %copy.25), calls=%async_computation.2 | async-start | bytes 3145728 | tf_op jit(solution)/shard_map/all_to_all | solution.py:59
  56.1 2.6 %copy.22 = bf16[1,384,2048]{1,2,0:T(8,128)(2,1)} copy(bf16[1,384,2048]{2,1,0:T(8,128)(2,1)} %param.9) | data formatting | bytes 3145728 | tf_op args[0]
  58.7 2.6 %copy.23 = bf16[384,16,128]{2,0,1:T(8,128)(2,1)} copy(bf16[384,16,128]{0,2,1:T(8,128)(2,1)} %bitcast.291) | data formatting | bytes 3145728 | tf_op jit(solution)/shard_map/all_to_all | solution.py:52
  61.3 16.5 %all-to-all-done.2 = bf16[384,16,128]{2,0,1:T(8,128)(2,1)S(1)} async-done(((bf16[384,16,128]{2,0,1:T(8,128)(2,1)}), bf16[384,16,128]{2,0,1:T(8,128)(2,1)S(1)}, u32[]{:S(2)}, u32[]{:S(2)}) %all-to-all-start.2) | async-done | bytes 1572896 | tf_op jit(solution)/shard_map/all_to_all | solution.py:59
  77.8 4.6 %all-to-all-start.1 = ((bf16[384,16,128]{2,0,1:T(8,128)(2,1)}), bf16[384,16,128]{2,0,1:T(8,128)(2,1)}, u32[]{:S(2)}, u32[]{:S(2)}) async-start(bf16[384,16,128]{2,0,1:T(8,128)(2,1)} %copy.23), calls=%async_computation.1 | async-start | bytes 3145728 | tf_op jit(solution)/shard_map/all_to_all | solution.py:52
  82.5 1.9 gather_fusion.7
  84.4 1.9 gather_fusion.5
  88.3 2.0 %gather_fusion.1 = bf16[16,384,128]{2,1,0:T(8,128)(2,1)} fusion(bf16[16,384,128]{2,1,0:T(8,128)(2,1)S(1)} %bitcast.289, s32[1024]{0:T(1024)S(1)} %pad_clamp_fusion.3), kind=kCustom, calls=%fused_computation.1.clone | custom fusion | bytes 3145792 | tf_op jit(solution)/shard_map/jit(_take)/gather | solution.py:25
  96.8 6.0 %all-to-all-done.1 = bf16[384,16,128]{2,0,1:T(8,128)(2,1)} async-done(((bf16[384,16,128]{2,0,1:T(8,128)(2,1)}), bf16[384,16,128]{2,0,1:T(8,128)(2,1)}, u32[]{:S(2)}, u32[]{:S(2)}) %all-to-all-start.1) | async-done | bytes 1572896 | tf_op jit(solution)/shard_map/all_to_all | solution.py:52
  102.7 3.4 %bitcast_reduce_fusion.1 = (f32[16,384]{1,0:T(8,128)S(1)}, f32[16,384,384]{2,1,0:T(8,128)S(1)}) fusion(pred[16]{0:T(512)(128)(4,1)S(1)} %get-tuple-element.31, bf16[384,16,128]{2,0,1:T(8,128)(2,1)} %all-to-all-done.1, bf16[16,384,128]{2,1,0:T(8,128)(2,1)} %gather_fusion.4, pred[16]{0:T(512)(128)(4,1)S(1)} %get-tuple-element.24), kind=kOutput, calls=%fused_computation.12 | convolution fusion | flops 611837952 | bytes 12607520 | tf_op jit(solution)/shard_map/athd,ashd->ahts/dot_general | solution.py:27
  106.2 6.5 %bitcast_reduce_fusion = (f32[16,384]{1,0:T(8,128)S(1)}, f32[16,384,384]{2,1,0:T(8,128)}) fusion(pred[16]{0:T(512)(128)(4,1)S(1)} %get-tuple-element.30, bf16[384,16,128]{2,0,1:T(8,128)(2,1)} %all-to-all-done.1, bf16[16,384,128]{2,1,0:T(8,128)(2,1)S(1)} %copy-done.6, pred[16]{0:T(512)(128)(4,1)S(1)} %get-tuple-element.22), kind=kOutput, calls=%fused_computation.9 | convolution fusion | flops 611837952 | bytes 12607520 | tf_op jit(solution)/shard_map/athd,ashd->ahts/dot_general | solution.py:27
  112.7 2.9 %bitcast_reduce_fusion.3 = (f32[16,384]{1,0:T(8,128)S(1)}, f32[16,384,384]{2,1,0:T(8,128)S(1)}) fusion(pred[16]{0:T(512)(128)(4,1)S(1)} %get-tuple-element.29, bf16[384,16,128]{2,0,1:T(8,128)(2,1)} %all-to-all-done.1, bf16[16,384,128]{2,1,0:T(8,128)(2,1)S(1)} %copy-done.5, pred[16]{0:T(512)(128)(4,1)S(1)} %get-tuple-element.26), kind=kOutput, calls=%fused_computation.18 | convolution fusion | flops 611837952 | bytes 12607520 | tf_op jit(solution)/shard_map/athd,ashd->ahts/dot_general | solution.py:27
  115.6 2.9 %bitcast_reduce_fusion.2 = (f32[16,384]{1,0:T(8,128)S(1)}, f32[16,384,384]{2,1,0:T(8,128)S(1)}) fusion(pred[16]{0:T(512)(128)(4,1)S(1)} %get-tuple-element.28, bf16[384,16,128]{2,0,1:T(8,128)(2,1)} %all-to-all-done.1, bf16[16,384,128]{2,1,0:T(8,128)(2,1)S(1)} %gather_fusion.2, pred[16]{0:T(512)(128)(4,1)S(1)} %get-tuple-element.15), kind=kOutput, calls=%fused_computation.15 | convolution fusion | flops 611837952 | bytes 12607520 | tf_op jit(solution)/shard_map/athd,ashd->ahts/dot_general | solution.py:27
  118.5 4.0 %fusion.4 = (f32[16,384]{1,0:T(8,128)S(1)}, f32[16,384]{1,0:T(8,128)S(1)}) fusion(f32[16,384,384]{2,1,0:T(8,128)S(1)} %get-tuple-element.37, f32[16,384]{1,0:T(8,128)S(1)} %get-tuple-element.36, pred[16]{0:T(512)(128)(4,1)S(1)} %get-tuple-element.29, f32[16,384]{1,0:T(8,128)S(1)} %get-tuple-element.12, f32[16,384,384]{2,1,0:T(8,128)S(1)} %get-tuple-element.39, ...), kind=kLoop, calls=%fused_computation.24 | loop fusion | flops 18862080 | bytes 18972704 | tf_op jit(solution)/shard_map/reduce_sum | solution.py:37
  122.5 6.7 %fusion.8 = (f32[16,384]{1,0:T(8,128)S(1)}, f32[16,384]{1,0:T(8,128)S(1)}) fusion(f32[16,384,384]{2,1,0:T(8,128)S(1)} %get-tuple-element.35, f32[16,384]{1,0:T(8,128)S(1)} %get-tuple-element.11, pred[16]{0:T(512)(128)(4,1)S(1)} %get-tuple-element.31, f32[16,384]{1,0:T(8,128)S(1)} %get-tuple-element.10, f32[16,384,384]{2,1,0:T(8,128)} %get-tuple-element.33, ...), kind=kLoop, calls=%fused_computation.28 | loop fusion | flops 18862080 | bytes 18972704 | tf_op jit(solution)/shard_map/reduce_sum | solution.py:37
  129.2 7.9 %fusion.12 = f32[16,128,384]{2,1,0:T(8,128)} fusion(f32[16,384,384]{2,1,0:T(8,128)} %get-tuple-element.33, f32[16,384]{1,0:T(8,128)S(1)} %get-tuple-element.10, pred[16]{0:T(512)(128)(4,1)S(1)} %get-tuple-element.30, bf16[16,384,128]{2,1,0:T(8,128)(2,1)S(1)} %copy-done.4, pred[16]{0:T(512)(128)(4,1)S(1)} %get-tuple-element.22), kind=kOutput, calls=%fused_computation.32 | convolution fusion | flops 614203392 | bytes 14180384 | tf_op jit(solution)/shard_map/ahts,ashd->athd/dot_general | solution.py:38
  137.2 3.9 %fusion.14 = f32[16,128,384]{2,1,0:T(8,128)} fusion(f32[16,384,384]{2,1,0:T(8,128)S(1)} %get-tuple-element.35, f32[16,384]{1,0:T(8,128)S(1)} %get-tuple-element.11, pred[16]{0:T(512)(128)(4,1)S(1)} %get-tuple-element.31, bf16[16,384,128]{2,1,0:T(8,128)(2,1)S(1)} %copy-done.3, pred[16]{0:T(512)(128)(4,1)S(1)} %get-tuple-element.24), kind=kOutput, calls=%fused_computation.33 | convolution fusion | flops 614203392 | bytes 14180384 | tf_op jit(solution)/shard_map/ahts,ashd->athd/dot_general | solution.py:38
  141.0 3.9 %fusion.16 = f32[16,128,384]{2,1,0:T(8,128)} fusion(f32[16,384,384]{2,1,0:T(8,128)S(1)} %get-tuple-element.39, f32[16,384]{1,0:T(8,128)S(1)} %get-tuple-element.12, pred[16]{0:T(512)(128)(4,1)S(1)} %get-tuple-element.28, bf16[16,384,128]{2,1,0:T(8,128)(2,1)S(1)} %copy-done.2, pred[16]{0:T(512)(128)(4,1)S(1)} %get-tuple-element.15), kind=kOutput, calls=%fused_computation.34 | convolution fusion | flops 614203392 | bytes 14180384 | tf_op jit(solution)/shard_map/ahts,ashd->athd/dot_general | solution.py:38
  144.9 6.7 %fusion.68 = bf16[16,384,128]{1,2,0:T(8,128)(2,1)} fusion(f32[16,384]{1,0:T(8,128)S(1)} %get-tuple-element.6, f32[16,128,384]{2,1,0:T(8,128)} %fusion.12, f32[16,384]{1,0:T(8,128)S(1)} %get-tuple-element.9, f32[16,128,384]{2,1,0:T(8,128)} %fusion.14, f32[16,384]{1,0:T(8,128)S(1)} %get-tuple-element.8, f32[16,128,384]{2,1,0:T(8,128)} %fusion.16, ...), kind=kOutput, calls=%fused_computation.95 | convolution fusion | flops 621281280 | bytes 22167584 | tf_op jit(solution)/shard_map/ahts,ashd->athd/dot_general | solution.py:38
  151.6 3.8 %all-to-all-start.3 = ((bf16[16,384,128]{1,2,0:T(8,128)(2,1)}), bf16[16,384,128]{1,2,0:T(8,128)(2,1)S(1)}, u32[]{:S(2)}, u32[]{:S(2)}) async-start(bf16[16,384,128]{1,2,0:T(8,128)(2,1)} %fusion.68), calls=%async_computation.3 | async-start | bytes 3145728 | tf_op jit(solution)/shard_map/all_to_all | solution.py:62
  155.5 22.1 %all-to-all-done.3 = bf16[16,384,128]{1,2,0:T(8,128)(2,1)S(1)} async-done(((bf16[16,384,128]{1,2,0:T(8,128)(2,1)}), bf16[16,384,128]{1,2,0:T(8,128)(2,1)S(1)}, u32[]{:S(2)}, u32[]{:S(2)}) %all-to-all-start.3) | async-done | bytes 1572896 | tf_op jit(solution)/shard_map/all_to_all | solution.py:62
  177.6 11.0 %fusion.36 = bf16[1,384,3072]{2,1,0:T(8,128)(2,1)} fusion(bf16[384,2048]{0,1:T(8,128)(2,1)S(1)} %bitcast.308, bf16[2048,3072]{1,0:T(8,128)(2,1)} %all-gather.2.cloned.1.call-done, f32[3072]{0:T(1024)S(1)} %bitcast.309), kind=kOutput, calls=%fused_computation.53 | convolution fusion | flops 4834197504 | bytes 16527360 | tf_op jit(solution)/shard_map/dot_general | solution.py:63
  (55 shorter events, 27.0 us)
Async XLA Ops:
  6.5 6.9 %copy-start = (bf16[1,384,2048]{2,1,0:T(8,128)(2,1)S(1)}, bf16[1,384,2048]{2,1,0:T(8,128)(2,1)}, u32[]{:S(2)}) copy-start(bf16[1,384,2048]{2,1,0:T(8,128)(2,1)} %param.10) | copy-start | bytes 4718596
  6.5 171.0 %all-gather.2.cloned.1.call-start = ((), (), s32[]{:S(2)}) async-start(), calls=%async_computation.4 | async-start | bytes 13369344 | tf_op jit(solution)/shard_map/all_gather | solution.py:65
  21.4 30.8 %all-to-all-start = ((bf16[16,384,128]{2,1,0:T(8,128)(2,1)}), bf16[16,384,128]{2,1,0:T(8,128)(2,1)S(1)}, u32[]{:S(2)}, u32[]{:S(2)}) async-start(bf16[16,384,128]{2,1,0:T(8,128)(2,1)} %fusion.81), calls=%async_computation | async-start | bytes 3145728 | tf_op jit(solution)/shard_map/all_to_all | solution.py:54
  52.2 25.6 %all-to-all-start.2 = ((bf16[384,16,128]{2,0,1:T(8,128)(2,1)}), bf16[384,16,128]{2,0,1:T(8,128)(2,1)S(1)}, u32[]{:S(2)}, u32[]{:S(2)}) async-start(bf16[384,16,128]{2,0,1:T(8,128)(2,1)} %copy.25), calls=%async_computation.2 | async-start | bytes 3145728 | tf_op jit(solution)/shard_map/all_to_all | solution.py:59
  61.3 21.1 %copy-start.8 = (s32[1,16,4]{1,2,0:T(4,128)S(1)}, s32[1,16,4]{1,2,0:T(4,128)}, u32[]{:S(2)}) copy-start(s32[1,16,4]{1,2,0:T(4,128)} %param.12) | copy-start | bytes 772
  61.3 21.2 %copy-start.9 = (s32[1,16]{1,0:T(1,128)S(1)}, s32[1,16]{1,0:T(1,128)}, u32[]{:S(2)}) copy-start(s32[1,16]{1,0:T(1,128)} %param.13) | copy-start | bytes 196
  77.8 24.9 %all-to-all-start.1 = ((bf16[384,16,128]{2,0,1:T(8,128)(2,1)}), bf16[384,16,128]{2,0,1:T(8,128)(2,1)}, u32[]{:S(2)}, u32[]{:S(2)}) async-start(bf16[384,16,128]{2,0,1:T(8,128)(2,1)} %copy.23), calls=%async_computation.1 | async-start | bytes 3145728 | tf_op jit(solution)/shard_map/all_to_all | solution.py:52
  102.7 3.5 %copy-start.6 = (bf16[16,384,128]{2,1,0:T(8,128)(2,1)S(1)}, bf16[16,384,128]{2,1,0:T(8,128)(2,1)}, u32[]{:S(2)}) copy-start(bf16[16,384,128]{2,1,0:T(8,128)(2,1)} %gather_fusion.6) | copy-start | bytes 4718596
  106.2 6.5 %copy-start.5 = (bf16[16,384,128]{2,1,0:T(8,128)(2,1)S(1)}, bf16[16,384,128]{2,1,0:T(8,128)(2,1)}, u32[]{:S(2)}) copy-start(bf16[16,384,128]{2,1,0:T(8,128)(2,1)} %gather_fusion) | copy-start | bytes 4718596
  122.5 6.7 %copy-start.4 = (bf16[16,384,128]{2,1,0:T(8,128)(2,1)S(1)}, bf16[16,384,128]{2,1,0:T(8,128)(2,1)}, u32[]{:S(2)}) copy-start(bf16[16,384,128]{2,1,0:T(8,128)(2,1)} %gather_fusion.7) | copy-start | bytes 4718596
  129.2 8.0 %copy-start.3 = (bf16[16,384,128]{2,1,0:T(8,128)(2,1)S(1)}, bf16[16,384,128]{2,1,0:T(8,128)(2,1)}, u32[]{:S(2)}) copy-start(bf16[16,384,128]{2,1,0:T(8,128)(2,1)} %gather_fusion.5) | copy-start | bytes 4718596
  137.1 3.9 %copy-start.2 = (bf16[16,384,128]{2,1,0:T(8,128)(2,1)S(1)}, bf16[16,384,128]{2,1,0:T(8,128)(2,1)}, u32[]{:S(2)}) copy-start(bf16[16,384,128]{2,1,0:T(8,128)(2,1)} %gather_fusion.3) | copy-start | bytes 4718596
  141.0 3.9 %copy-start.1 = (bf16[16,384,128]{2,1,0:T(8,128)(2,1)S(1)}, bf16[16,384,128]{2,1,0:T(8,128)(2,1)}, u32[]{:S(2)}) copy-start(bf16[16,384,128]{2,1,0:T(8,128)(2,1)} %gather_fusion.1) | copy-start | bytes 4718596
  151.6 3.9 %copy-start.7 = (bf16[1,3072]{1,0:T(2,128)(2,1)S(1)}, bf16[1,3072]{1,0:T(2,128)(2,1)}, u32[]{:S(2)}) copy-start(bf16[1,3072]{1,0:T(2,128)(2,1)} %param.15) | copy-start | bytes 18436
  151.6 26.0 %all-to-all-start.3 = ((bf16[16,384,128]{1,2,0:T(8,128)(2,1)}), bf16[16,384,128]{1,2,0:T(8,128)(2,1)S(1)}, u32[]{:S(2)}, u32[]{:S(2)}) async-start(bf16[16,384,128]{1,2,0:T(8,128)(2,1)} %fusion.68), calls=%async_computation.3 | async-start | bytes 3145728 | tf_op jit(solution)/shard_map/all_to_all | solution.py:62
Sparse Core Ops, SparseCore 0:
  9.2 76.8 all-gather.1
